TPU v7x, 512 devices: a whole 4x4x16 slice. The times are simulated.
512 devices in a mesh: section: 4 (over x_hi, core), expert: 16 (over z), tensor: 8 (over y, x_lo).
Axes of the slice: x: 4 (x_hi: 2, x_lo: 2; x = x_hi * 2 + x_lo), y: 4, z: 16, core: 2. Of those that a mesh axis runs over, the one named last changes fastest.
Arguments:
- tokens: bfloat16 [8192, 5120], P(('section', 'expert'), 'tensor'), may hold values from -6 to 6
- norm_gain: float32 [5120], P('tensor'), may hold values from 0.1 to 1.9
- router: bfloat16 [5120, 16], P('tensor'), may hold values from -0.078125 to 0.078125
- expert_ids: int32 [8192, 1], P(('section', 'expert')), may hold values from 0 to 15; in each aligned block of 128 rows (0 to 127, 128 to 255, ...) at most 16 rows name the same one
- gate_proj: bfloat16 [16, 5120, 4096], P('expert', None, ('section', 'tensor')), may hold values from -0.078125 to 0.078125
- up_proj: bfloat16 [16, 5120, 4096], P('expert', None, ('section', 'tensor')), may hold values from -0.078125 to 0.078125
- down_proj: bfloat16 [16, 4096, 5120], P('expert', 'section', 'tensor'), may hold values from -0.09375 to 0.09375
Outputs:
- moe_out: bfloat16 [8192, 5120], P(('section', 'expert'), 'tensor')
Inputs may be any that keep to these rules, and one draw needn't show every extreme that they name: `expert_ids`: within each aligned block of 128 tokens (the tokens of one group of devices along section and expert) no expert is named by more than 16 tokens, a bound that some block reaches.
All inputs are finite; a program needn't handle non-finite values.
Results may differ from a plain program's by a relative error of at most 0.017.
Values may be sent and summed in bfloat16 or wider, within the bound.
No kernel may reach another device: no remote copies, remote signals or barrier semaphores. Data moves between devices by JAX's collectives and lax.ppermute only.
A program may use at most 64 MiB of HBM per device.

v0:
```python
import jax
import jax.numpy as jnp
from jax import lax
from jax.sharding import PartitionSpec as P

D = 5120
EPSILON = 1e-05


def from_everyone(array, axis):
    count = lax.axis_size(axis)
    return lax.all_to_all(
        jnp.broadcast_to(array[None], (count, *array.shape)), axis, 0, 0, tiled=True
    )


def of_everyone(array, axis):
    return from_everyone(array, axis).sum(axis=0)


def joined_along(parts, dim):
    parts = jnp.moveaxis(parts, 0, dim)
    shape = parts.shape
    return parts.reshape(*shape[:dim], shape[dim] * shape[dim + 1], *shape[dim + 2 :])


def collect(array, axis, dim):
    return joined_along(from_everyone(array, axis), dim)


def in_blocks(array, dim, count):
    shape = array.shape
    parts = array.reshape(*shape[:dim], count, shape[dim] // count, *shape[dim + 1 :])
    return jnp.moveaxis(parts, dim, 0)


def summed_on_arrival(array, axis, dim):
    parts = in_blocks(array, dim, lax.axis_size(axis))
    arrived = lax.all_to_all(parts, axis, split_axis=0, concat_axis=0, tiled=True)
    return arrived.sum(axis=0)


def slot_table(expert_ids, experts, capacity):
    chosen = expert_ids[:, 0]
    member = (chosen[:, None] == jnp.arange(experts, dtype=jnp.int32)[None, :]).astype(jnp.int32)
    earlier = jnp.cumsum(member, axis=0) - member
    placed = chosen * capacity + jnp.sum(earlier * member, axis=1)
    placing = placed[:, None] == jnp.arange(experts * capacity, dtype=jnp.int32)[None, :]
    return (member, placing)


def normalize(tokens, norm_gain, squares):
    values = tokens.astype(jnp.float32)
    return (values * lax.rsqrt(squares / D + EPSILON) * norm_gain).astype(jnp.bfloat16)


def on_device(tokens, norm_gain, router, expert_ids, gate_proj, up_proj, down_proj):
    row_count = tokens.shape[0]
    experts = router.shape[1]
    capacity = 2 * row_count // experts
    values = tokens.astype(jnp.float32)
    squares = of_everyone(jnp.sum(values * values, axis=1, keepdims=True), "tensor")
    normed = normalize(tokens, norm_gain, squares)
    logits = of_everyone(jnp.dot(normed, router, preferred_element_type=jnp.float32), "tensor")
    member, placing = slot_table(expert_ids, experts, capacity)
    score = jax.nn.sigmoid(jnp.sum(jnp.where(member > 0, logits, jnp.float32(0.0)), axis=1))
    routed = (normed.astype(jnp.float32) * score[:, None]).astype(jnp.bfloat16)
    placing = placing.astype(jnp.bfloat16)
    outgoing = jnp.einsum("tc,td->cd", placing, routed, preferred_element_type=jnp.float32).astype(
        jnp.bfloat16
    )
    arrived = lax.all_to_all(outgoing, "expert", split_axis=0, concat_axis=0, tiled=True)
    gate_cols = gate_proj[0]
    up_cols = up_proj[0]
    down_rows = down_proj[0]
    widened = collect(arrived, "tensor", 1)
    piece = lax.all_gather(widened, "section", axis=0, tiled=True)
    gate = jnp.dot(piece, gate_cols, preferred_element_type=jnp.float32)
    upper = jnp.dot(piece, up_cols, preferred_element_type=jnp.float32)
    hidden = (jax.nn.silu(gate) * upper).astype(jnp.bfloat16)
    full_hidden = collect(hidden, "tensor", 1)
    summed = summed_on_arrival(
        jnp.dot(full_hidden, down_rows, preferred_element_type=jnp.float32), "section", 0
    )
    returned = lax.all_to_all(
        summed.astype(jnp.bfloat16), "expert", split_axis=0, concat_axis=0, tiled=True
    )
    result = jnp.einsum("tc,cd->td", placing, returned, preferred_element_type=jnp.float32)
    return result.astype(jnp.bfloat16)


def solution(mesh):
    in_specs = (
        P(("section", "expert"), "tensor"),
        P("tensor"),
        P("tensor", None),
        P(("section", "expert"), None),
        P("expert", None, ("section", "tensor")),
        P("expert", None, ("section", "tensor")),
        P("expert", "section", "tensor"),
    )
    out_specs = P(("section", "expert"), "tensor")
    return jax.shard_map(
        on_device, mesh=mesh, in_specs=in_specs, out_specs=out_specs, check_vma=False
    )
```

profile of v0, /device:TPU:64, one launch (start us, length us, event | category | flops | bytes accessed | tf_op | source)
XLA Modules:
  0.0 304.4 jit_solution(2847538108800103751)
XLA Ops:
  6.5 0.0 copy-start
  6.5 1.1 fusion.12
  7.7 0.6 broadcast_in_dim.14
  8.3 5.4 %all-to-all-start = ((f32[8,128,1]{1,2,0:T(1,128)}), f32[8,128,1]{1,2,0:T(1,128)S(1)}, u32[]{:S(2)}, u32[]{:S(2)}) async-start(f32[8,128,1]{1,2,0:T(1,128)} %broadcast_in_dim.14), calls=%async_computation | async-start | bytes 8192 | tf_op jit(solution)/shard_map/all_to_all | solution.py:12
  13.7 0.7 fusion.18
  14.4 0.2 reduce_window_sum.11
  14.6 0.8 select_reduce_fusion.1
  15.4 4.3 %all-to-all-done = f32[8,128,1]{1,2,0:T(1,128)S(1)} async-done(((f32[8,128,1]{1,2,0:T(1,128)}), f32[8,128,1]{1,2,0:T(1,128)S(1)}, u32[]{:S(2)}, u32[]{:S(2)}) %all-to-all-start) | async-done | bytes 4128 | tf_op jit(solution)/shard_map/all_to_all | solution.py:12
  19.8 1.1 fusion.19
  20.9 0.7 broadcast_in_dim.15
  21.6 3.4 %all-to-all-start.1 = ((f32[8,128,16]{1,2,0:T(8,128)}), f32[8,128,16]{1,2,0:T(8,128)S(1)}, u32[]{:S(2)}, u32[]{:S(2)}) async-start(f32[8,128,16]{1,2,0:T(8,128)} %broadcast_in_dim.15), calls=%async_computation.1 | async-start | bytes 131072 | tf_op jit(solution)/shard_map/all_to_all | solution.py:12
  25.0 0.0 all-gather.2.cloned.1.call-start
  25.0 0.7 fusion.22
  25.7 5.6 %all-to-all-done.1 = f32[8,128,16]{1,2,0:T(8,128)S(1)} async-done(((f32[8,128,16]{1,2,0:T(8,128)}), f32[8,128,16]{1,2,0:T(8,128)S(1)}, u32[]{:S(2)}, u32[]{:S(2)}) %all-to-all-start.1) | async-done | bytes 65568 | tf_op jit(solution)/shard_map/all_to_all | solution.py:12
  31.3 0.1 copy.11
  31.4 0.8 select_reduce_fusion
  32.2 1.3 convolution_convert_fusion
  33.5 32.8 %all_to_all.43 = bf16[16,16,640]{2,1,0:T(8,128)(2,1)S(1)} all-to-all(bf16[16,16,640]{2,1,0:T(8,128)(2,1)S(1)} %bitcast.37), channel_id=1, replica_groups=mesh['section'=4,'expert'=16,'tensor'=8] {'expert'}, dimensions={0} | all-to-all | bytes 655360 | tf_op jit(solution)/shard_map/all_to_all | solution.py:72
  66.3 0.2 copy.12
  66.5 0.2 broadcast_in_dim.18
  66.7 27.6 %all_to_all.44 = bf16[8,256,640]{1,2,0:T(8,128)(2,1)} all-to-all(bf16[8,256,640]{1,2,0:T(8,128)(2,1)S(1)} %broadcast_in_dim.18), channel_id=1, replica_groups=mesh['section'=4,'expert'=16,'tensor'=8] {'tensor'}, dimensions={0} | all-to-all | bytes 5242880 | tf_op jit(solution)/shard_map/all_to_all | solution.py:12
  94.2 0.0 copy-start.2
  94.2 0.0 all-gather.2.cloned.1.call-update
  94.3 82.6 %all-gather.2.cloned.1.call-done = bf16[1024,5120]{0,1:T(8,128)(2,1)} async-done(((bf16[256,5120]{0,1:T(8,128)(2,1)}), bf16[1024,5120]{0,1:T(8,128)(2,1)}) %all-gather.2.cloned.1.call-update) | async-done | bytes 10485776 | tf_op jit(solution)/shard_map/all_gather | solution.py:77
  176.8 0.0 copy-done.2
  176.8 0.0 copy-start.1
  176.8 0.0 copy-start.3
  176.8 5.8 %fusion.4 = f32[1024,128]{1,0:T(8,128)S(1)} fusion(bf16[1024,5120]{0,1:T(8,128)(2,1)} %all-gather.2.cloned.1.call-done, bf16[1,5120,128]{2,1,0:T(8,128)(2,1)S(1)} %copy-done.2), kind=kOutput, calls=%fused_computation.4 | convolution fusion | flops 1342177280 | bytes 12320768 | tf_op jit(solution)/shard_map/dot_general | solution.py:78
  182.7 1.2 copy-done.1
  183.9 0.3 copy-done.3
  184.2 2.9 fusion.9
  187.1 0.3 broadcast_in_dim.19
  187.4 31.4 %all_to_all.45 = bf16[8,1024,128]{2,1,0:T(8,128)(2,1)S(1)} all-to-all(bf16[8,1024,128]{2,1,0:T(8,128)(2,1)S(1)} %broadcast_in_dim.19), channel_id=1, replica_groups=mesh['section'=4,'expert'=16,'tensor'=8] {'tensor'}, dimensions={0} | all-to-all | bytes 4194304 | tf_op jit(solution)/shard_map/all_to_all | solution.py:12
  218.8 1.4 copy.13
  220.2 2.3 dot_general.24
  222.5 0.0 copy-done
  222.5 3.4 %fusion = f32[4,256,640]{2,1,0:T(8,128)S(1)} fusion(bf16[4,256,1024]{2,1,0:T(8,128)(2,1)} %dot_general.24, bf16[1,1024,640]{2,1,0:T(8,128)(2,1)S(1)} %copy-done), kind=kOutput, calls=%fused_computation | convolution fusion | flops 1342177280 | bytes 6029312 | tf_op jit(solution)/shard_map/dot_general | solution.py:83
  225.9 36.1 %all_to_all.46 = f32[4,256,640]{2,1,0:T(8,128)} all-to-all(f32[4,256,640]{2,1,0:T(8,128)S(1)} %fusion), channel_id=1, replica_groups=mesh['section'=4,'expert'=16,'tensor'=8] {'section'}, dimensions={0} | all-to-all | bytes 5242880 | tf_op jit(solution)/shard_map/all_to_all | solution.py:39
  262.0 1.9 reduce_sum.62
  263.9 32.7 %all_to_all.47 = bf16[16,16,640]{2,1,0:T(8,128)(2,1)S(1)} all-to-all(bf16[16,16,640]{2,1,0:T(8,128)(2,1)S(1)} %bitcast.36), channel_id=1, replica_groups=mesh['section'=4,'expert'=16,'tensor'=8] {'expert'}, dimensions={0} | all-to-all | bytes 655360 | tf_op jit(solution)/shard_map/all_to_all | solution.py:85
  296.6 0.9 convolution_convert_fusion.1
  (4 shorter events, 0.1 us)
Async XLA Ops:
  6.5 216.0 %copy-start = (bf16[1,1024,640]{2,1,0:T(8,128)(2,1)S(1)}, bf16[1,1024,640]{2,1,0:T(8,128)(2,1)}, u32[]{:S(2)}) copy-start(bf16[1,1024,640]{2,1,0:T(8,128)(2,1)} %param.13) | copy-start | bytes 3932164
  8.3 11.5 %all-to-all-start = ((f32[8,128,1]{1,2,0:T(1,128)}), f32[8,128,1]{1,2,0:T(1,128)S(1)}, u32[]{:S(2)}, u32[]{:S(2)}) async-start(f32[8,128,1]{1,2,0:T(1,128)} %broadcast_in_dim.14), calls=%async_computation | async-start | bytes 8192 | tf_op jit(solution)/shard_map/all_to_all | solution.py:12
  21.6 9.6 %all-to-all-start.1 = ((f32[8,128,16]{1,2,0:T(8,128)}), f32[8,128,16]{1,2,0:T(8,128)S(1)}, u32[]{:S(2)}, u32[]{:S(2)}) async-start(f32[8,128,16]{1,2,0:T(8,128)} %broadcast_in_dim.15), calls=%async_computation.1 | async-start | bytes 131072 | tf_op jit(solution)/shard_map/all_to_all | solution.py:12
  25.0 151.8 %all-gather.2.cloned.1.call-start = ((), (), s32[]{:S(2)}) async-start(), calls=%async_computation.7 | async-start | bytes 13107200 | tf_op jit(solution)/shard_map/all_gather | solution.py:77
  94.2 82.6 %copy-start.2 = (bf16[1,5120,128]{2,1,0:T(8,128)(2,1)S(1)}, bf16[1,5120,128]{2,1,0:T(8,128)(2,1)}, u32[]{:S(2)}) copy-start(bf16[1,5120,128]{2,1,0:T(8,128)(2,1)} %param.11) | copy-start | bytes 3932164
  176.8 7.0 %copy-start.1 = (bf16[1024,5120]{0,1:T(8,128)(2,1)S(1)}, bf16[1024,5120]{0,1:T(8,128)(2,1)}, u32[]{:S(2)}) copy-start(bf16[1024,5120]{0,1:T(8,128)(2,1)} %all-gather.2.cloned.1.call-done) | copy-start | bytes 31457284
  176.8 7.3 %copy-start.3 = (bf16[1,5120,128]{2,1,0:T(8,128)(2,1)S(1)}, bf16[1,5120,128]{2,1,0:T(8,128)(2,1)}, u32[]{:S(2)}) copy-start(bf16[1,5120,128]{2,1,0:T(8,128)(2,1)} %param.12) | copy-start | bytes 3932164
Sparse Core Ops, SparseCore 0:
  94.4 82.4 all-gather.1
where the time goes:
time: 305 us; the launch traced here: 304 us
  blocking collectives  161 us (53%)
  waiting for transfers between devices  92.5 us (30%)
  matrix products  15.5 us (5%)
  between operations  13.5 us (4%)
  starting transfers between devices  8.79 us (3%)
  local copies, waits for them, and re-layouts  7.22 us (2%)
  other arithmetic  6.3 us (2%)
    all_gather x1, waiting for transfers between devices, on_device(): piece = lax.all_gather(widened, 'section', axis=0, tiled=True)  82.6 us
    all_to_all x2, blocking collectives, from_everyone(): lax.all_to_all(jnp.broadcast_to(array[None], (count, *array.shape)), axis...  59 us
    all_to_all x1, blocking collectives, summed_on_arrival(): lax.all_to_all(parts, axis, split_axis=0, concat_axis=0, tiled=True)  36.1 us
    all_to_all x1, blocking collectives, on_device(): lax.all_to_all(outgoing, 'expert', split_axis=0, concat_axis=0, tiled=True)  32.8 us
    all_to_all x1, blocking collectives, on_device(): lax.all_to_all(summed.astype(jnp.bfloat16), 'expert', split_axis=0, conca...  32.7 us
    all_to_all x2, waiting for transfers between devices, from_everyone(): lax.all_to_all(jnp.broadcast_to(array[None], (count, *array.shape)), axis...  9.89 us
    all_to_all x2, starting transfers between devices, from_everyone(): lax.all_to_all(jnp.broadcast_to(array[None], (count, *array.shape)), axis...  8.75 us
  transfers between devices with their start and end apart: 3, of which 3 were waited for; matrix products, arithmetic and copies ran while one was open for 1% of the time, Pallas kernels for 0%

commit v1 on v0

--- a/solution.py
+++ b/solution.py
@@ -74,7 +74,10 @@
     up_cols = up_proj[0]
     down_rows = down_proj[0]
     widened = collect(arrived, "tensor", 1)
-    piece = lax.all_gather(widened, "section", axis=0, tiled=True)
+    n_dev = lax.axis_size("section")
+    pieces = jnp.stack([widened for _ in range(n_dev)])
+    pieces = lax.all_to_all(pieces, "section", split_axis=0, concat_axis=0)
+    piece = jnp.concatenate(pieces, axis=0)
     gate = jnp.dot(piece, gate_cols, preferred_element_type=jnp.float32)
     upper = jnp.dot(piece, up_cols, preferred_element_type=jnp.float32)
     hidden = (jax.nn.silu(gate) * upper).astype(jnp.bfloat16)

time: 305 us -> 336 us (1.10)
  blocking collectives: 161 us -> 280 us
  waiting for transfers between devices: 92.5 us -> 9.94 us
  between operations: 13.5 us -> 0.11 us
  local copies, waits for them, and re-layouts: 7.22 us -> 17.2 us
    all_to_all x0 -> x1, blocking collectives: none -> 121 us  [on_device(): pieces = lax.all_to_all(pieces, 'section', split_axis=0, concat_axis=0)]
    all_gather x1 -> x0, waiting for transfers between devices: 82.6 us -> none  [on_device(): piece = lax.all_gather(widened, 'section', axis=0, tiled=True)]
    another operation x0 -> x2, local copies, waits for them, and re-layouts: none -> 11.5 us  [on_device(): pieces = jnp.stack([widened for _ in range(n_dev)])]
  transfers between devices with their start and end apart: 3 -> 2, of which waited for: 3 -> 2; matrix products, arithmetic and copies ran while one was open for 1% -> 1% of each run, Pallas kernels for 0% -> 0%
where the time goes in v1:
time: 336 us; the launch traced here: 335 us
  blocking collectives  280 us (83%)
  local copies, waits for them, and re-layouts  17.2 us (5%)
  matrix products  12.5 us (4%)
  waiting for transfers between devices  9.94 us (3%)
  starting transfers between devices  8.75 us (3%)
  other arithmetic  6.3 us (2%)
    all_to_all x1, blocking collectives, on_device(): pieces = lax.all_to_all(pieces, 'section', split_axis=0, concat_axis=0)  121 us
    all_to_all x2, blocking collectives, from_everyone(): lax.all_to_all(jnp.broadcast_to(array[None], (count, *array.shape)), axis...  56.8 us
    all_to_all x1, blocking collectives, summed_on_arrival(): lax.all_to_all(parts, axis, split_axis=0, concat_axis=0, tiled=True)  36.1 us
    all_to_all x1, blocking collectives, on_device(): lax.all_to_all(outgoing, 'expert', split_axis=0, concat_axis=0, tiled=True)  32.8 us
    all_to_all x1, blocking collectives, on_device(): lax.all_to_all(summed.astype(jnp.bfloat16), 'expert', split_axis=0, conca...  32.8 us
    another operation x2, local copies, waits for them, and re-layouts, on_device(): pieces = jnp.stack([widened for _ in range(n_dev)])  11.5 us
    all_to_all x2, waiting for transfers between devices, from_everyone(): lax.all_to_all(jnp.broadcast_to(array[None], (count, *array.shape)), axis...  9.94 us
    all_to_all x2, starting transfers between devices, from_everyone(): lax.all_to_all(jnp.broadcast_to(array[None], (count, *array.shape)), axis...  8.75 us
  transfers between devices with their start and end apart: 2, of which 2 were waited for; matrix products, arithmetic and copies ran while one was open for 1% of the time, Pallas kernels for 0%

profile of v1, /device:TPU:64, one launch (start us, length us, event | category | flops | bytes accessed | tf_op | source)
XLA Modules:
  0.0 334.8 jit_solution(1177243464983830592)
XLA Ops:
  0.0 0.0 copy-start
  0.0 1.1 fusion.12
  1.1 0.6 broadcast_in_dim.14
  1.7 5.4 %all-to-all-start = ((f32[8,128,1]{1,2,0:T(1,128)}), f32[8,128,1]{1,2,0:T(1,128)S(1)}, u32[]{:S(2)}, u32[]{:S(2)}) async-start(f32[8,128,1]{1,2,0:T(1,128)} %broadcast_in_dim.14), calls=%async_computation | async-start | bytes 8192 | tf_op jit(solution)/shard_map/all_to_all | solution.py:12
  7.1 0.7 fusion.18
  7.9 0.2 reduce_window_sum.11
  8.1 0.8 select_reduce_fusion.1
  8.9 4.3 %all-to-all-done = f32[8,128,1]{1,2,0:T(1,128)S(1)} async-done(((f32[8,128,1]{1,2,0:T(1,128)}), f32[8,128,1]{1,2,0:T(1,128)S(1)}, u32[]{:S(2)}, u32[]{:S(2)}) %all-to-all-start) | async-done | bytes 4128 | tf_op jit(solution)/shard_map/all_to_all | solution.py:12
  13.3 1.1 fusion.19
  14.4 0.7 broadcast_in_dim.15
  15.1 3.4 %all-to-all-start.1 = ((f32[8,128,16]{1,2,0:T(8,128)}), f32[8,128,16]{1,2,0:T(8,128)S(1)}, u32[]{:S(2)}, u32[]{:S(2)}) async-start(f32[8,128,16]{1,2,0:T(8,128)} %broadcast_in_dim.15), calls=%async_computation.1 | async-start | bytes 131072 | tf_op jit(solution)/shard_map/all_to_all | solution.py:12
  18.4 0.7 fusion.22
  19.1 5.6 %all-to-all-done.1 = f32[8,128,16]{1,2,0:T(8,128)S(1)} async-done(((f32[8,128,16]{1,2,0:T(8,128)}), f32[8,128,16]{1,2,0:T(8,128)S(1)}, u32[]{:S(2)}, u32[]{:S(2)}) %all-to-all-start.1) | async-done | bytes 65568 | tf_op jit(solution)/shard_map/all_to_all | solution.py:12
  24.7 0.1 copy.13
  24.8 0.8 select_reduce_fusion
  25.7 1.3 convolution_convert_fusion
  27.0 32.8 %all_to_all.48 = bf16[16,16,640]{2,1,0:T(8,128)(2,1)S(1)} all-to-all(bf16[16,16,640]{2,1,0:T(8,128)(2,1)S(1)} %bitcast.40), channel_id=1, replica_groups=mesh['section'=4,'expert'=16,'tensor'=8] {'expert'}, dimensions={0} | all-to-all | bytes 655360 | tf_op jit(solution)/shard_map/all_to_all | solution.py:72
  59.8 0.2 copy.14
  60.0 0.2 broadcast_in_dim.18
  60.1 27.5 %all_to_all.49 = bf16[8,256,640]{1,2,0:T(8,128)(2,1)} all-to-all(bf16[8,256,640]{1,2,0:T(8,128)(2,1)S(1)} %broadcast_in_dim.18), channel_id=1, replica_groups=mesh['section'=4,'expert'=16,'tensor'=8] {'tensor'}, dimensions={0} | all-to-all | bytes 5242880 | tf_op jit(solution)/shard_map/all_to_all | solution.py:12
  87.7 4.5 %copy.15 = bf16[256,5120]{1,0:T(8,128)(2,1)} copy(bf16[256,5120]{0,1:T(8,128)(2,1)} %bitcast.37) | data formatting | bytes 5242880 | tf_op jit(solution)/shard_map/stack;reshape | solution.py:78
  92.1 7.0 %stack.3 = bf16[4,256,5120]{2,1,0:T(8,128)(2,1)} broadcast(bf16[256,5120]{1,0:T(8,128)(2,1)} %copy.15), dimensions={1,2} | broadcast | bytes 13107200 | tf_op jit(solution)/shard_map/stack | solution.py:78
  99.2 0.0 copy-start.1
  99.2 121.5 %all_to_all.50 = bf16[4,256,5120]{2,1,0:T(8,128)(2,1)S(1)} all-to-all(bf16[4,256,5120]{2,1,0:T(8,128)(2,1)} %stack.3), channel_id=1, replica_groups=mesh['section'=4,'expert'=16,'tensor'=8] {'section'}, dimensions={0} | all-to-all | bytes 20971520 | tf_op jit(solution)/shard_map/all_to_all | solution.py:79
  220.7 0.0 copy-done.1
  220.7 0.0 copy-start.2
  220.7 2.9 fusion.4
  223.5 0.0 copy-done.2
  223.6 2.9 fusion.9
  226.4 0.3 broadcast_in_dim.19
  226.7 29.3 %all_to_all.51 = bf16[8,1024,128]{2,1,0:T(8,128)(2,1)S(1)} all-to-all(bf16[8,1024,128]{2,1,0:T(8,128)(2,1)S(1)} %broadcast_in_dim.19), channel_id=1, replica_groups=mesh['section'=4,'expert'=16,'tensor'=8] {'tensor'}, dimensions={0} | all-to-all | bytes 4194304 | tf_op jit(solution)/shard_map/all_to_all | solution.py:12
  256.0 1.4 copy.16
  257.4 2.3 dot_general.24
  259.7 0.0 copy-done
  259.7 3.4 %fusion = f32[4,256,640]{2,1,0:T(8,128)S(1)} fusion(bf16[4,256,1024]{2,1,0:T(8,128)(2,1)} %dot_general.24, bf16[1,1024,640]{2,1,0:T(8,128)(2,1)S(1)} %copy-done), kind=kOutput, calls=%fused_computation | convolution fusion | flops 1342177280 | bytes 6029312 | tf_op jit(solution)/shard_map/dot_general | solution.py:86
  263.1 36.1 %all_to_all.52 = f32[4,256,640]{2,1,0:T(8,128)} all-to-all(f32[4,256,640]{2,1,0:T(8,128)S(1)} %fusion), channel_id=1, replica_groups=mesh['section'=4,'expert'=16,'tensor'=8] {'section'}, dimensions={0} | all-to-all | bytes 5242880 | tf_op jit(solution)/shard_map/all_to_all | solution.py:39
  299.2 1.9 reduce_sum.62
  301.1 32.8 %all_to_all.53 = bf16[16,16,640]{2,1,0:T(8,128)(2,1)S(1)} all-to-all(bf16[16,16,640]{2,1,0:T(8,128)(2,1)S(1)} %bitcast.39), channel_id=1, replica_groups=mesh['section'=4,'expert'=16,'tensor'=8] {'expert'}, dimensions={0} | all-to-all | bytes 655360 | tf_op jit(solution)/shard_map/all_to_all | solution.py:88
  333.8 0.9 convolution_convert_fusion.1
  (4 shorter events, 0.1 us)
Async XLA Ops:
  0.0 259.7 %copy-start = (bf16[1,1024,640]{2,1,0:T(8,128)(2,1)S(1)}, bf16[1,1024,640]{2,1,0:T(8,128)(2,1)}, u32[]{:S(2)}) copy-start(bf16[1,1024,640]{2,1,0:T(8,128)(2,1)} %param.13) | copy-start | bytes 3932164
  1.7 11.5 %all-to-all-start = ((f32[8,128,1]{1,2,0:T(1,128)}), f32[8,128,1]{1,2,0:T(1,128)S(1)}, u32[]{:S(2)}, u32[]{:S(2)}) async-start(f32[8,128,1]{1,2,0:T(1,128)} %broadcast_in_dim.14), calls=%async_computation | async-start | bytes 8192 | tf_op jit(solution)/shard_map/all_to_all | solution.py:12
  15.1 9.6 %all-to-all-start.1 = ((f32[8,128,16]{1,2,0:T(8,128)}), f32[8,128,16]{1,2,0:T(8,128)S(1)}, u32[]{:S(2)}, u32[]{:S(2)}) async-start(f32[8,128,16]{1,2,0:T(8,128)} %broadcast_in_dim.15), calls=%async_computation.1 | async-start | bytes 131072 | tf_op jit(solution)/shard_map/all_to_all | solution.py:12
  99.2 121.5 %copy-start.1 = (bf16[1,5120,128]{2,1,0:T(8,128)(2,1)S(1)}, bf16[1,5120,128]{2,1,0:T(8,128)(2,1)}, u32[]{:S(2)}) copy-start(bf16[1,5120,128]{2,1,0:T(8,128)(2,1)} %param.11) | copy-start | bytes 3932164
  220.7 2.9 copy-start.2
